TPU v7x, 32 devices: a whole 2x2x4 slice. The times are simulated.
32 devices in a mesh: fsdp: 4 (over y, core), replica: 8 (over z, x).
Axes of the slice: x: 2, y: 2, z: 4, core: 2. Of those that a mesh axis runs over, the one named last changes fastest.
Arguments:
- tokens: bfloat16 [16384, 1024], P(('fsdp', 'replica')), may hold values from -6 to 6
- seq_lengths: int32 [32, 4], P(('fsdp', 'replica')), may hold values from 0 to 512, as said below
- attention_gain: bfloat16 [1024], P('fsdp'), may hold values from 0.5 to 1.5
- query_weight: bfloat16 [1024, 2048], P('fsdp'), may hold values from -0.1875 to 0.1875
- key_matrix: bfloat16 [1024, 1024], P('fsdp'), may hold values from -0.1875 to 0.1875
- value_matrix: bfloat16 [1024, 1024], P('fsdp'), may hold values from -0.1875 to 0.1875
- query_norm_gain: bfloat16 [128], P('fsdp'), may hold values from 0.5 to 1.5
- key_gain: bfloat16 [128], P('fsdp'), may hold values from 0.5 to 1.5
- out_weight: bfloat16 [2048, 1024], P('fsdp'), may hold values from -1 to 1
- feed_gain: bfloat16 [1024], P('fsdp'), may hold values from 0.5 to 1.5
- gate_weight: bfloat16 [1024, 3072], P('fsdp'), may hold values from -0.1875 to 0.1875
- up_weight: bfloat16 [1024, 3072], P('fsdp'), may hold values from -0.1875 to 0.1875
- down_weight: bfloat16 [3072, 1024], P('fsdp'), may hold values from -0.109375 to 0.109375
- cotangent: bfloat16 [16384, 1024], P(('fsdp', 'replica')), may hold values from -6 to 6
Outputs:
- output: bfloat16 [16384, 1024], P(('fsdp', 'replica'))
- grad_tokens: bfloat16 [16384, 1024], P(('fsdp', 'replica'))
- grad_attention_gain: float32 [1024], P('fsdp')
- grad_query_weight: float32 [1024, 2048], P('fsdp')
- grad_key_weight: float32 [1024, 1024], P('fsdp')
- grad_value_weight: float32 [1024, 1024], P('fsdp')
- grad_query_gain: float32 [128], P('fsdp')
- grad_key_gain: float32 [128], P('fsdp')
- grad_out_weight: float32 [2048, 1024], P('fsdp')
- grad_feed_gain: float32 [1024], P('fsdp')
- grad_gate_weight: float32 [1024, 3072], P('fsdp')
- grad_up_weight: float32 [1024, 3072], P('fsdp')
- grad_down_weight: float32 [3072, 1024], P('fsdp')
Inputs may be any that keep to these rules, and one draw needn't show every extreme that they name: `seq_lengths`: row b lists the lengths of up to 4 sequences of the device whose buffer is b; the first entry is at least 1, unused slots are 0 and stand only after used ones. Each sequence fills ceil(length / 128) blocks of 128 slots, one after another from slot 0, and a row's sequences fill at most 4 blocks. Some row holds a single sequence of 512 tokens.
All inputs are finite; a program needn't handle non-finite values.
Results may differ from a plain program's by a relative error of at most 0.015.
Values may be sent and summed in bfloat16 or wider, within the bound.
A program may use at most 256 MiB of HBM per device.

v0:
```python
import math

import jax
import jax.numpy as jnp
from jax import lax
from jax.sharding import PartitionSpec as P

QUERY_HEADS = 16
KEY_VALUE_HEADS = 8
HEAD_SIZE = 128
BLOCK = 128


norm_eps = 1e-06
rope_base = 1000000.0


def layout(lengths_row, token_count):
    blocks = (lengths_row + BLOCK - 1) // BLOCK
    ends = jnp.cumsum(blocks) * BLOCK
    starts = ends - blocks * BLOCK
    places = jnp.arange(token_count, dtype=jnp.int32)
    inside = (places[:, None] >= starts[None, :]) & (
        places[:, None] < starts[None, :] + lengths_row[None, :]
    )
    numbers = jnp.arange(lengths_row.shape[0], dtype=jnp.int32) + 1
    segment = jnp.sum(jnp.where(inside, numbers[None, :], 0), axis=1)
    position = jnp.sum(jnp.where(inside, places[:, None] - starts[None, :], 0), axis=1)
    return (segment, position)


def rope_tables(position):
    half = HEAD_SIZE // 2
    freq = jnp.exp(-math.log(rope_base) * 2.0 * jnp.arange(half, dtype=jnp.float32) / HEAD_SIZE)
    angle = position.astype(jnp.float32)[:, None] * freq[None, :]
    return (jnp.cos(angle)[:, None, :], jnp.sin(angle)[:, None, :])


def apply_rotary(value_rows, cosine_table, sine_table):
    half = HEAD_SIZE // 2
    first_half = value_rows[..., :half]
    second_half = value_rows[..., half:]
    return jnp.concatenate(
        [
            first_half * cosine_table - second_half * sine_table,
            second_half * cosine_table + first_half * sine_table,
        ],
        axis=-1,
    )


def unit_scale(value_rows):
    inverse = lax.rsqrt(jnp.mean(value_rows * value_rows, axis=-1, keepdims=True) + norm_eps)
    return (value_rows * inverse, inverse)


def norm_back(grad, unit, inverse, gain):
    scaled = grad * gain
    return inverse * (scaled - unit * jnp.mean(scaled * unit, axis=-1, keepdims=True))


def contract_rows(left, right):
    return lax.dot_general(
        left, right, (((0,), (0,)), ((), ())), preferred_element_type=jnp.float32
    )


def product_with_transpose(left, right):
    return lax.dot_general(
        left, right, (((1,), (1,)), ((), ())), preferred_element_type=jnp.float32
    )


def masked_scores(query_rows, key_rows, seg_rows, seg_keys, first):
    scores = jnp.einsum(
        "qgrd,kgd->grqk", query_rows, key_rows, preferred_element_type=jnp.float32
    ) / math.sqrt(HEAD_SIZE)
    rows_at = first + jnp.arange(query_rows.shape[0], dtype=jnp.int32)
    cols_at = jnp.arange(key_rows.shape[0], dtype=jnp.int32)
    allowed = (seg_rows[:, None] == seg_keys[None, :]) & (cols_at[None, :] <= rows_at[:, None])
    return jnp.where(allowed[None, None], scores, -1e30)


def local(
    tokens,
    seq_lengths,
    attention_gain,
    query_weight,
    key_matrix,
    value_matrix,
    query_norm_gain,
    key_gain,
    out_weight,
    feed_gain,
    gate_weight,
    up_weight,
    down_weight,
    cotangent,
):
    token_count = tokens.shape[0]
    head_groups = QUERY_HEADS // KEY_VALUE_HEADS
    rows_block = min(256, token_count)
    blocks = token_count // rows_block
    segment, position = layout(seq_lengths[0], token_count)
    cosine_table, sine_table = rope_tables(position)
    attention_set = (
        lax.all_gather(attention_gain, "fsdp", axis=0, tiled=True),
        lax.all_gather(query_weight, "fsdp", axis=0, tiled=True),
        lax.all_gather(key_matrix, "fsdp", axis=0, tiled=True),
        lax.all_gather(value_matrix, "fsdp", axis=0, tiled=True),
        lax.all_gather(query_norm_gain, "fsdp", axis=0, tiled=True),
        lax.all_gather(key_gain, "fsdp", axis=0, tiled=True),
        lax.all_gather(out_weight, "fsdp", axis=0, tiled=True),
    )
    first_gain, query_full, key_complete, value_full, query_scale, key_scale, out_full = (
        attention_set
    )
    first_gain = first_gain.astype(jnp.float32)
    query_scale = query_scale.astype(jnp.float32)
    key_scale = key_scale.astype(jnp.float32)
    inputs = tokens.astype(jnp.float32)
    unit_first, inverse_first = unit_scale(inputs)
    hidden_state = (unit_first * first_gain).astype(jnp.bfloat16)
    query_raw = jnp.dot(hidden_state, query_full, preferred_element_type=jnp.float32).reshape(
        token_count, QUERY_HEADS, HEAD_SIZE
    )
    key_unnormed = jnp.dot(hidden_state, key_complete, preferred_element_type=jnp.float32).reshape(
        token_count, KEY_VALUE_HEADS, HEAD_SIZE
    )
    value_reduced = jnp.dot(hidden_state, value_full, preferred_element_type=jnp.float32).astype(
        jnp.bfloat16
    )
    value_reduced = value_reduced.reshape(token_count, KEY_VALUE_HEADS, HEAD_SIZE)
    query_unit, query_inverse = unit_scale(query_raw)
    key_unit, key_inverse = unit_scale(key_unnormed)
    query_low = (
        apply_rotary(query_unit * query_scale, cosine_table, sine_table)
        .astype(jnp.bfloat16)
        .reshape(token_count, KEY_VALUE_HEADS, head_groups, HEAD_SIZE)
    )
    key_low = apply_rotary(key_unit * key_scale, cosine_table, sine_table).astype(jnp.bfloat16)
    block_outs = []
    tops = []
    totals = []
    for number in range(blocks):
        start = number * rows_block
        finish = start + rows_block
        scores = masked_scores(
            query_low[start:finish],
            key_low[:finish],
            segment[start:finish],
            segment[:finish],
            start,
        )
        top = jnp.max(scores, axis=-1, keepdims=True)
        weight = jnp.exp(scores - top)
        total = jnp.sum(weight, axis=-1, keepdims=True)
        probs_low = (weight / total).astype(jnp.bfloat16)
        block_outs.append(
            jnp.einsum(
                "grqk,kgd->qgrd",
                probs_low,
                value_reduced[:finish],
                preferred_element_type=jnp.float32,
            )
        )
        tops.append(top)
        totals.append(total)
    mixed_low = (
        jnp.concatenate(block_outs, axis=0)
        .reshape(token_count, QUERY_HEADS * HEAD_SIZE)
        .astype(jnp.bfloat16)
    )
    middle = inputs + jnp.dot(mixed_low, out_full, preferred_element_type=jnp.float32)
    feed_set = (
        lax.all_gather(feed_gain, "fsdp", axis=0, tiled=True),
        lax.all_gather(gate_weight, "fsdp", axis=0, tiled=True),
        lax.all_gather(up_weight, "fsdp", axis=0, tiled=True),
        lax.all_gather(down_weight, "fsdp", axis=0, tiled=True),
    )
    second_gain, gate_full, up_full, down_full = feed_set
    second_gain = second_gain.astype(jnp.float32)
    unit_second, inverse_second = unit_scale(middle)
    hidden_second = (unit_second * second_gain).astype(jnp.bfloat16)
    gate = jnp.dot(hidden_second, gate_full, preferred_element_type=jnp.float32)
    up_value = jnp.dot(hidden_second, up_full, preferred_element_type=jnp.float32)
    sigma = jax.nn.sigmoid(gate)
    silu_value = gate * sigma
    activation_low = (silu_value * up_value).astype(jnp.bfloat16)
    result = middle + jnp.dot(activation_low, down_full, preferred_element_type=jnp.float32)
    output = result.astype(jnp.bfloat16)
    live = (segment > 0).astype(jnp.float32)
    grad_result = cotangent.astype(jnp.float32) * live[:, None]
    feed_back = (
        lax.all_gather(feed_gain, "fsdp", axis=0, tiled=True),
        lax.all_gather(gate_weight, "fsdp", axis=0, tiled=True),
        lax.all_gather(up_weight, "fsdp", axis=0, tiled=True),
        lax.all_gather(down_weight, "fsdp", axis=0, tiled=True),
    )
    gate_back, up_back, down_back = (feed_back[1], feed_back[2], feed_back[3])
    grad_result_low = grad_result.astype(jnp.bfloat16)
    grad_down = contract_rows(activation_low, grad_result_low)
    grad_act = product_with_transpose(grad_result_low, down_back)
    grad_silu = grad_act * up_value
    gate_grad_low = (grad_silu * (sigma + gate * sigma * (1.0 - sigma))).astype(jnp.bfloat16)
    up_grad_low = (grad_act * silu_value).astype(jnp.bfloat16)
    grad_gate = contract_rows(hidden_second, gate_grad_low)
    grad_up = contract_rows(hidden_second, up_grad_low)
    grad_hidden_second = product_with_transpose(gate_grad_low, gate_back) + product_with_transpose(
        up_grad_low, up_back
    )
    grad_second_gain = jnp.sum(grad_hidden_second * unit_second, axis=0)
    grad_middle = grad_result + norm_back(
        grad_hidden_second, unit_second, inverse_second, second_gain
    )
    feed_shares = (
        lax.psum_scatter(
            grad_second_gain.astype(jnp.bfloat16), "fsdp", scatter_dimension=0, tiled=True
        ).astype(jnp.float32),
        lax.psum_scatter(
            grad_gate.astype(jnp.bfloat16), "fsdp", scatter_dimension=0, tiled=True
        ).astype(jnp.float32),
        lax.psum_scatter(
            grad_up.astype(jnp.bfloat16), "fsdp", scatter_dimension=0, tiled=True
        ).astype(jnp.float32),
        lax.psum_scatter(
            grad_down.astype(jnp.bfloat16), "fsdp", scatter_dimension=0, tiled=True
        ).astype(jnp.float32),
    )
    attention_back = (
        lax.all_gather(attention_gain, "fsdp", axis=0, tiled=True),
        lax.all_gather(query_weight, "fsdp", axis=0, tiled=True),
        lax.all_gather(key_matrix, "fsdp", axis=0, tiled=True),
        lax.all_gather(value_matrix, "fsdp", axis=0, tiled=True),
        lax.all_gather(query_norm_gain, "fsdp", axis=0, tiled=True),
        lax.all_gather(key_gain, "fsdp", axis=0, tiled=True),
        lax.all_gather(out_weight, "fsdp", axis=0, tiled=True),
    )
    query_back, key_back, value_back, output_backward = (
        attention_back[1],
        attention_back[2],
        attention_back[3],
        attention_back[6],
    )
    middle_reduced = grad_middle.astype(jnp.bfloat16)
    grad_out = contract_rows(mixed_low, middle_reduced)
    grad_mixed_low = (
        product_with_transpose(middle_reduced, output_backward)
        .astype(jnp.bfloat16)
        .reshape(token_count, KEY_VALUE_HEADS, head_groups, HEAD_SIZE)
    )
    key_gradient_total = jnp.zeros((token_count, KEY_VALUE_HEADS, HEAD_SIZE), jnp.float32)
    value_gradient_total = jnp.zeros((token_count, KEY_VALUE_HEADS, HEAD_SIZE), jnp.float32)
    query_grads = []
    for number in range(blocks):
        start = number * rows_block
        finish = start + rows_block
        scores = masked_scores(
            query_low[start:finish],
            key_low[:finish],
            segment[start:finish],
            segment[:finish],
            start,
        )
        probs = jnp.exp(scores - tops[number]) / totals[number]
        probs_low = probs.astype(jnp.bfloat16)
        grad_slice = grad_mixed_low[start:finish]
        value_gradient_total = value_gradient_total.at[:finish].add(
            jnp.einsum("grqk,qgrd->kgd", probs_low, grad_slice, preferred_element_type=jnp.float32)
        )
        grad_probs = jnp.einsum(
            "qgrd,kgd->grqk", grad_slice, value_reduced[:finish], preferred_element_type=jnp.float32
        )
        grad_scores = probs * (grad_probs - jnp.sum(probs * grad_probs, axis=-1, keepdims=True))
        scores_low = grad_scores.astype(jnp.bfloat16)
        query_grads.append(
            jnp.einsum(
                "grqk,kgd->qgrd", scores_low, key_low[:finish], preferred_element_type=jnp.float32
            )
            / math.sqrt(HEAD_SIZE)
        )
        key_gradient_total = key_gradient_total.at[:finish].add(
            jnp.einsum(
                "grqk,qgrd->kgd",
                scores_low,
                query_low[start:finish],
                preferred_element_type=jnp.float32,
            )
            / math.sqrt(HEAD_SIZE)
        )
    grad_query_rot = jnp.concatenate(query_grads, axis=0).reshape(
        token_count, QUERY_HEADS, HEAD_SIZE
    )
    grad_query_norm = apply_rotary(grad_query_rot, cosine_table, -sine_table)
    grad_query_scale = jnp.sum(grad_query_norm * query_unit, axis=(0, 1))
    query_grad_low = norm_back(grad_query_norm, query_unit, query_inverse, query_scale)
    query_grad_low = query_grad_low.astype(jnp.bfloat16).reshape(
        token_count, QUERY_HEADS * HEAD_SIZE
    )
    grad_key_norm = apply_rotary(key_gradient_total, cosine_table, -sine_table)
    grad_key_scale = jnp.sum(grad_key_norm * key_unit, axis=(0, 1))
    key_gradient_reduced = norm_back(grad_key_norm, key_unit, key_inverse, key_scale)
    key_gradient_reduced = key_gradient_reduced.astype(jnp.bfloat16).reshape(
        token_count, KEY_VALUE_HEADS * HEAD_SIZE
    )
    value_gradient_reduced = value_gradient_total.astype(jnp.bfloat16).reshape(
        token_count, KEY_VALUE_HEADS * HEAD_SIZE
    )
    grad_query = contract_rows(hidden_state, query_grad_low)
    grad_key = contract_rows(hidden_state, key_gradient_reduced)
    grad_value = contract_rows(hidden_state, value_gradient_reduced)
    grad_hidden = (
        product_with_transpose(query_grad_low, query_back)
        + product_with_transpose(key_gradient_reduced, key_back)
        + product_with_transpose(value_gradient_reduced, value_back)
    )
    grad_first_gain = jnp.sum(grad_hidden * unit_first, axis=0)
    grad_inputs = grad_middle + norm_back(grad_hidden, unit_first, inverse_first, first_gain)
    attention_shares = (
        lax.psum_scatter(
            grad_first_gain.astype(jnp.bfloat16), "fsdp", scatter_dimension=0, tiled=True
        ).astype(jnp.float32),
        lax.psum_scatter(
            grad_query.astype(jnp.bfloat16), "fsdp", scatter_dimension=0, tiled=True
        ).astype(jnp.float32),
        lax.psum_scatter(
            grad_key.astype(jnp.bfloat16), "fsdp", scatter_dimension=0, tiled=True
        ).astype(jnp.float32),
        lax.psum_scatter(
            grad_value.astype(jnp.bfloat16), "fsdp", scatter_dimension=0, tiled=True
        ).astype(jnp.float32),
        lax.psum_scatter(
            grad_query_scale.astype(jnp.bfloat16), "fsdp", scatter_dimension=0, tiled=True
        ).astype(jnp.float32),
        lax.psum_scatter(
            grad_key_scale.astype(jnp.bfloat16), "fsdp", scatter_dimension=0, tiled=True
        ).astype(jnp.float32),
        lax.psum_scatter(
            grad_out.astype(jnp.bfloat16), "fsdp", scatter_dimension=0, tiled=True
        ).astype(jnp.float32),
    )
    summed = lax.psum(
        (
            attention_shares[0],
            attention_shares[1],
            attention_shares[2],
            attention_shares[3],
            attention_shares[4],
            attention_shares[5],
            attention_shares[6],
            feed_shares[0],
            feed_shares[1],
            feed_shares[2],
            feed_shares[3],
        ),
        "replica",
    )
    attention_shares = summed[:7]
    feed_shares = summed[7:]
    factor = 1.0 / math.sqrt(token_count * lax.axis_size("fsdp") * lax.axis_size("replica"))
    return (
        output,
        grad_inputs.astype(jnp.bfloat16),
        attention_shares[0] * factor,
        attention_shares[1] * factor,
        attention_shares[2] * factor,
        attention_shares[3] * factor,
        attention_shares[4] * factor,
        attention_shares[5] * factor,
        attention_shares[6] * factor,
        feed_shares[0] * factor,
        feed_shares[1] * factor,
        feed_shares[2] * factor,
        feed_shares[3] * factor,
    )


def solution(mesh):
    in_specs = (
        P(("fsdp", "replica"), None),
        P(("fsdp", "replica"), None),
        P("fsdp"),
        P("fsdp", None),
        P("fsdp", None),
        P("fsdp", None),
        P("fsdp"),
        P("fsdp"),
        P("fsdp", None),
        P("fsdp"),
        P("fsdp", None),
        P("fsdp", None),
        P("fsdp", None),
        P(("fsdp", "replica"), None),
    )
    out_specs = (
        P(("fsdp", "replica"), None),
        P(("fsdp", "replica"), None),
        P("fsdp"),
        P("fsdp", None),
        P("fsdp", None),
        P("fsdp", None),
        P("fsdp"),
        P("fsdp"),
        P("fsdp", None),
        P("fsdp"),
        P("fsdp", None),
        P("fsdp", None),
        P("fsdp", None),
    )
    return jax.shard_map(local, mesh=mesh, in_specs=in_specs, out_specs=out_specs, check_vma=False)
```

profile of v0, /device:TPU:0, one launch (start us, length us, event | category | flops | bytes accessed | tf_op | source)
XLA Modules:
  0.0 1318.7 jit_solution(598369429349631361)
XLA Ops:
  13.0 6.0 all-gather
  21.1 8.1 all-reduce.10
  30.4 5.1 all-gather.1
  36.7 1.8 fusion.78
  38.6 2.9 fusion.95
  43.3 1.7 copy.151
  45.0 14.2 %all-gather.10.cloned.1.call-done = bf16[1024,1024]{1,0:T(8,128)(2,1)} async-done(((bf16[256,1024]{1,0:T(8,128)(2,1)}), bf16[1024,1024]{1,0:T(8,128)(2,1)}) %all-gather.10.cloned.1.call-update) | async-done | bytes 2097168 | tf_op jit(solution)/shard_map/all_gather | solution.py:110
  59.2 2.9 convolution_convert_fusion.9
  66.1 1.8 subtract_convert_fusion.1
  67.9 27.4 %all-gather.14.cloned.1.call-done = bf16[1024,2048]{1,0:T(8,128)(2,1)} async-done(((bf16[256,2048]{1,0:T(8,128)(2,1)}), bf16[1024,2048]{1,0:T(8,128)(2,1)}) %all-gather.14.cloned.1.call-update) | async-done | bytes 4194320 | tf_op jit(solution)/shard_map/all_gather | solution.py:108
  95.3 4.9 fusion.93
  105.0 2.0 multiply_multiply_fusion
  107.0 1.8 subtract_convert_fusion
  112.5 5.6 fusion.103
  118.1 8.5 fusion.102
  126.6 3.1 fusion.49
  129.7 1.8 copy-done.9
  134.3 5.5 multiply_reduce_fusion.5
  142.4 36.7 %all-gather.18.cloned.1.call-done = bf16[1024,3072]{1,0:T(8,128)(2,1)} async-done(((bf16[256,3072]{1,0:T(8,128)(2,1)}), bf16[1024,3072]{1,0:T(8,128)(2,1)}) %all-gather.18.cloned.1.call-update) | async-done | bytes 6291472 | tf_op jit(solution)/shard_map/all_gather | solution.py:177
  179.1 9.9 fusion.108
  189.0 37.9 %all-gather.20.cloned.1.call-done = bf16[1024,3072]{1,0:T(8,128)(2,1)} async-done(((bf16[256,3072]{1,0:T(8,128)(2,1)}), bf16[1024,3072]{1,0:T(8,128)(2,1)}) %all-gather.20.cloned.1.call-update) | async-done | bytes 6291472 | tf_op jit(solution)/shard_map/all_gather | solution.py:178
  226.9 9.5 fusion.109
  236.4 38.5 %all-gather.22.cloned.1.call-done = bf16[3072,1024]{1,0:T(8,128)(2,1)} async-done(((bf16[768,1024]{1,0:T(8,128)(2,1)}), bf16[3072,1024]{1,0:T(8,128)(2,1)}) %all-gather.22.cloned.1.call-update) | async-done | bytes 6291472 | tf_op jit(solution)/shard_map/all_gather | solution.py:179
  274.9 11.5 multiply_convert_fusion
  286.4 8.1 fusion.110
  294.5 3.8 multiply_reduce_fusion.2
  300.5 2.4 convolution_convert_fusion.5
  304.5 2.3 copy.226
  306.8 8.5 fusion.2
  315.3 2.3 copy.225
  317.6 3.5 fusion.11
  324.1 1.8 copy-done.10
  325.9 4.7 fusion.4
  333.7 2.8 fusion.63
  337.4 1.7 mul.533
  342.2 2.8 convolution_convert_fusion.7
  346.2 3.0 convolution_bitcast_fusion.1
  349.3 5.6 fusion.34
  355.9 2.8 convolution_convert_fusion.6
  360.2 1.9 multiply_bitcast_fusion.1
  365.1 1.9 fusion.98
  367.0 5.3 copy.222
  372.2 3.9 copy.223
  376.1 4.5 multiply_subtract_fusion
  380.8 3.7 multiply_reduce_fusion
  388.3 7.3 fusion.10
  397.0 4.4 convolution_convert_fusion.4
  403.0 5.9 convolution_convert_fusion.3
  409.0 8.4 convolution_convert_fusion.2
  417.5 9.0 convolution_convert_fusion.1
  426.8 8.4 convolution_convert_fusion
  436.5 3.3 fusion.111
  442.8 4.2 fusion.28
  447.0 6.6 all-reduce.9
  453.9 3.3 fusion.27
  457.2 7.2 add_convert_fusion.1
  464.4 40.8 %reduce-scatter.14.cloned.1.call-done = bf16[512,1024]{1,0:T(8,128)(2,1)} async-done(((bf16[2048,1024]{1,0:T(8,128)(2,1)}), bf16[512,1024]{1,0:T(8,128)(2,1)}) %reduce-scatter.14.cloned.1.call-update) | async-done | bytes 1048592 | tf_op jit(solution)/shard_map/reduce_scatter | solution.py:338
  505.2 60.8 %reduce-scatter.16.cloned.1.call-done = bf16[256,3072]{1,0:T(8,128)(2,1)} async-done(((bf16[1024,3072]{1,0:T(8,128)(2,1)}), bf16[256,3072]{1,0:T(8,128)(2,1)}) %reduce-scatter.16.cloned.1.call-update) | async-done | bytes 1572880 | tf_op jit(solution)/shard_map/reduce_scatter | solution.py:220
  566.0 61.1 %reduce-scatter.18.cloned.1.call-done = bf16[256,3072]{1,0:T(8,128)(2,1)} async-done(((bf16[1024,3072]{1,0:T(8,128)(2,1)}), bf16[256,3072]{1,0:T(8,128)(2,1)}) %reduce-scatter.18.cloned.1.call-update) | async-done | bytes 1572880 | tf_op jit(solution)/shard_map/reduce_scatter | solution.py:223
  627.1 60.8 %reduce-scatter.20.cloned.1.call-done = bf16[768,1024]{1,0:T(8,128)(2,1)} async-done(((bf16[3072,1024]{1,0:T(8,128)(2,1)}), bf16[768,1024]{1,0:T(8,128)(2,1)}) %reduce-scatter.20.cloned.1.call-update) | async-done | bytes 1572880 | tf_op jit(solution)/shard_map/reduce_scatter | solution.py:226
  687.9 606.6 %all-reduce.12 = (f32[256]{0:T(256)S(1)}, f32[256,2048]{1,0:T(8,128)}, f32[256,1024]{1,0:T(8,128)}, f32[256,1024]{1,0:T(8,128)}, f32[32]{0:T(128)S(1)}, /*index=...) all-reduce(f32[256]{0:T(256)S(1)} %dynamic-slice_convert_fusion.3, ...), channel_id=1, replica_groups=mesh['fsdp'=4,'replica'=8] {'replica'}, use_global_device_ids=true, to_apply=%region_19.20 | all-reduce | flops 3932736 | bytes 23597568 | tf_op jit(solution)/shard_map/psum | solution.py:342
  1294.4 4.3 broadcast_multiply_fusion
  1298.7 1.9 broadcast_multiply_fusion.1
  1300.6 1.9 broadcast_multiply_fusion.2
  (253 shorter events, 69.2 us)
Async XLA Ops:
  7.2 31.4 %all-gather.12.cloned.1.call-start = ((), (), s32[]{:S(2)}) async-start(), calls=%async_computation.8 | async-start | bytes 2621440 | tf_op jit(solution)/shard_map/all_gather | solution.py:109
  7.9 51.3 %all-gather.10.cloned.1.call-start = ((), (), s32[]{:S(2)}) async-start(), calls=%async_computation.7 | async-start | bytes 2621440 | tf_op jit(solution)/shard_map/all_gather | solution.py:110
  8.7 86.6 %all-gather.14.cloned.1.call-start = ((), (), s32[]{:S(2)}) async-start(), calls=%async_computation.9 | async-start | bytes 5242880 | tf_op jit(solution)/shard_map/all_gather | solution.py:108
  9.4 124.9 %all-gather.16.cloned.1.call-start = ((), (), s32[]{:S(2)}) async-start(), calls=%async_computation.10 | async-start | bytes 5242880 | tf_op jit(solution)/shard_map/all_gather | solution.py:113
  10.0 3.0 copy-start.64
  10.0 9.0 copy-start.20
  10.0 169.1 %all-gather.18.cloned.1.call-start = ((), (), s32[]{:S(2)}) async-start(), calls=%async_computation.11 | async-start | bytes 7864320 | tf_op jit(solution)/shard_map/all_gather | solution.py:177
  10.6 8.7 copy-start.58
  10.6 9.9 copy-start.65
  10.6 10.2 copy-start.66
  10.6 19.8 %copy-start.67 = (bf16[256]{0:T(256)(128)(2,1)S(1)}, bf16[256]{0:T(256)(128)(2,1)}, u32[]{:S(2)}) copy-start(bf16[256]{0:T(256)(128)(2,1)} %param.35) | copy-start | bytes 1540
  10.6 216.3 %all-gather.20.cloned.1.call-start = ((), (), s32[]{:S(2)}) async-start(), calls=%async_computation.12 | async-start | bytes 7864320 | tf_op jit(solution)/shard_map/all_gather | solution.py:178
  11.2 263.7 %all-gather.22.cloned.1.call-start = ((), (), s32[]{:S(2)}) async-start(), calls=%async_computation.13 | async-start | bytes 7864320 | tf_op jit(solution)/shard_map/all_gather | solution.py:179
  12.0 452.5 %reduce-scatter.10.cloned.1.call-start = ((), (), s32[]{:S(2)}) async-start(), calls=%async_computation.15 | async-start | bytes 2621440 | tf_op jit(solution)/shard_map/reduce_scatter | solution.py:326
  19.0 40.3 %copy-start.47 = (f32[4,1,256]{2,1,0:T(1,128)}, f32[4,1,256]{2,1,0:T(1,128)S(1)}, u32[]{:S(2)}) copy-start(f32[4,1,256]{2,1,0:T(1,128)S(1)} %convert_element_type.211) | copy-start | bytes 12292
  19.3 40.0 %copy-start.50 = (f32[512]{0:T(512)}, f32[512]{0:T(512)S(1)}, u32[]{:S(2)}) copy-start(f32[512]{0:T(512)S(1)} %add_rsqrt_fusion.3) | copy-start | bytes 6148
  29.7 9.0 copy-start.55
  62.1 2.2 copy-start.43
  62.1 3.0 copy-start.56
  102.2 2.8 copy-start.53
  126.6 4.9 copy-start.9
  126.6 5.1 copy-start.36
  126.6 5.1 copy-start.46
  134.3 6.9 copy-start.44
  189.0 85.9 %copy-start.52 = (f32[512]{0:T(512)S(1)}, f32[512]{0:T(512)}, u32[]{:S(2)}) copy-start(f32[512]{0:T(512)} %compare_convert_fusion) | copy-start | bytes 6148
  286.4 8.1 copy-start.71
  286.4 8.1 copy-start.70
  286.4 8.1 copy-start.12
  286.4 8.1 copy-start.60
  294.5 3.8 copy-start.34
  298.3 2.2 copy-start.62
  300.5 2.4 copy-start.14
  315.3 2.3 copy-start.45
  317.6 3.9 copy-start.19
  321.5 4.5 copy-start.10
  325.9 4.8 copy-start.37
  337.4 2.3 copy-start.16
  337.4 2.3 copy-start.49
  339.7 2.5 copy-start.21
  339.7 2.5 copy-start.48
  339.7 2.5 copy-start.51
  345.0 4.2 copy-start.38
  345.0 119.4 %reduce-scatter.12.cloned.1.call-start = ((), (), s32[]{:S(2)}) async-start(), calls=%async_computation.16 | async-start | bytes 2621440 | tf_op jit(solution)/shard_map/reduce_scatter | solution.py:329
  349.2 6.6 copy-start.22
  358.7 105.8 %reduce-scatter.8.cloned.1.call-start = ((), (), s32[]{:S(2)}) async-start(), calls=%async_computation.14 | async-start | bytes 5242880 | tf_op jit(solution)/shard_map/reduce_scatter | solution.py:323
  360.2 2.6 copy-start.3
  360.2 3.0 copy-start.8
  372.2 3.9 copy-start.27
  376.1 4.7 copy-start.1
  376.1 4.7 copy-start.18
  385.6 2.7 copy-start.7
  388.3 8.7 copy-start.23
  401.5 103.7 %reduce-scatter.14.cloned.1.call-start = ((), (), s32[]{:S(2)}) async-start(), calls=%async_computation.17 | async-start | bytes 5242880 | tf_op jit(solution)/shard_map/reduce_scatter | solution.py:338
  409.0 157.0 %reduce-scatter.16.cloned.1.call-start = ((), (), s32[]{:S(2)}) async-start(), calls=%async_computation.18 | async-start | bytes 7864320 | tf_op jit(solution)/shard_map/reduce_scatter | solution.py:220
  417.4 209.6 %reduce-scatter.18.cloned.1.call-start = ((), (), s32[]{:S(2)}) async-start(), calls=%async_computation.19 | async-start | bytes 7864320 | tf_op jit(solution)/shard_map/reduce_scatter | solution.py:223
  426.5 261.3 %reduce-scatter.20.cloned.1.call-start = ((), (), s32[]{:S(2)}) async-start(), calls=%async_computation.20 | async-start | bytes 7864320 | tf_op jit(solution)/shard_map/reduce_scatter | solution.py:226
  436.5 3.4 copy-start.63
  436.5 3.4 copy-start.69
  439.9 2.9 copy-start.61
  453.9 3.3 copy-start.13
  453.9 3.3 copy-start.72
  1294.4 4.3 copy-start.25
  1300.6 2.5 copy-start.31
  1303.2 2.3 copy-start.30
  (23 other events, 33.7 us)
Sparse Core Ops, SparseCore 0:
  9.6 25.4 all-gather.11
  36.6 22.5 all-gather.9
  60.8 34.4 all-gather.13
  96.7 34.4 all-gather.15
  132.6 46.3 all-gather.17
  180.5 46.3 all-gather.19
  228.5 46.3 all-gather.21
  345.1 31.4 reduce-scatter.9
  379.3 31.4 reduce-scatter.11
  413.2 44.7 reduce-scatter.7
  460.6 44.5 reduce-scatter.13
  507.6 58.3 reduce-scatter.15
  568.7 58.3 reduce-scatter.17
  629.5 58.3 reduce-scatter.19
where the time goes:
time: 1330 us; the launch traced here: 1320 us
  blocking collectives  632 us (48%)
  waiting for transfers between devices  383 us (29%)
  matrix products  163 us (12%)
  other arithmetic  64.1 us (5%)
  local copies, waits for them, and re-layouts  58.3 us (4%)
  between operations  17.2 us (1%)
    psum x1, blocking collectives, local(): lax.psum((attention_shares[0], attention_shares[1], attention_shares[2],...  607 us
    reduce_scatter x1, waiting for transfers between devices, local(): lax.psum_scatter(grad_up.astype(jnp.bfloat16), 'fsdp', scatter_dimension=...  61.1 us
    reduce_scatter x1, waiting for transfers between devices, local(): lax.psum_scatter(grad_gate.astype(jnp.bfloat16), 'fsdp', scatter_dimensio...  60.8 us
    reduce_scatter x1, waiting for transfers between devices, local(): lax.psum_scatter(grad_down.astype(jnp.bfloat16), 'fsdp', scatter_dimensio...  60.8 us
    dot_general x7, matrix products, contract_rows(): lax.dot_general(left, right, (((0,), (0,)), ((), ())), preferred_element_...  41.7 us
    reduce_scatter x1, waiting for transfers between devices, local(): lax.psum_scatter(grad_out.astype(jnp.bfloat16), 'fsdp', scatter_dimension...  40.8 us
    unnamed x161, local copies, waits for them, and re-layouts  40.2 us
    all_gather x1, waiting for transfers between devices, local(): lax.all_gather(down_weight, 'fsdp', axis=0, tiled=True)  38.5 us
  transfers between devices with their start and end apart: 14, of which 9 were waited for; matrix products, arithmetic and copies ran while one was open for 14% of the time, Pallas kernels for 0%

commit v1 on v0

--- a/solution.py
+++ b/solution.py
@@ -216,16 +216,16 @@
     feed_shares = (
         lax.psum_scatter(
             grad_second_gain.astype(jnp.bfloat16), "fsdp", scatter_dimension=0, tiled=True
-        ).astype(jnp.float32),
+        ),
         lax.psum_scatter(
             grad_gate.astype(jnp.bfloat16), "fsdp", scatter_dimension=0, tiled=True
-        ).astype(jnp.float32),
+        ),
         lax.psum_scatter(
             grad_up.astype(jnp.bfloat16), "fsdp", scatter_dimension=0, tiled=True
-        ).astype(jnp.float32),
+        ),
         lax.psum_scatter(
             grad_down.astype(jnp.bfloat16), "fsdp", scatter_dimension=0, tiled=True
-        ).astype(jnp.float32),
+        ),
     )
     attention_back = (
         lax.all_gather(attention_gain, "fsdp", axis=0, tiled=True),
@@ -319,25 +319,25 @@
     attention_shares = (
         lax.psum_scatter(
             grad_first_gain.astype(jnp.bfloat16), "fsdp", scatter_dimension=0, tiled=True
-        ).astype(jnp.float32),
+        ),
         lax.psum_scatter(
             grad_query.astype(jnp.bfloat16), "fsdp", scatter_dimension=0, tiled=True
-        ).astype(jnp.float32),
+        ),
         lax.psum_scatter(
             grad_key.astype(jnp.bfloat16), "fsdp", scatter_dimension=0, tiled=True
-        ).astype(jnp.float32),
+        ),
         lax.psum_scatter(
             grad_value.astype(jnp.bfloat16), "fsdp", scatter_dimension=0, tiled=True
-        ).astype(jnp.float32),
+        ),
         lax.psum_scatter(
             grad_query_scale.astype(jnp.bfloat16), "fsdp", scatter_dimension=0, tiled=True
-        ).astype(jnp.float32),
+        ),
         lax.psum_scatter(
             grad_key_scale.astype(jnp.bfloat16), "fsdp", scatter_dimension=0, tiled=True
-        ).astype(jnp.float32),
+        ),
         lax.psum_scatter(
             grad_out.astype(jnp.bfloat16), "fsdp", scatter_dimension=0, tiled=True
-        ).astype(jnp.float32),
+        ),
     )
     summed = lax.psum(
         (
@@ -355,6 +355,7 @@
         ),
         "replica",
     )
+    summed = tuple(share.astype(jnp.float32) for share in summed)
     attention_shares = summed[:7]
     feed_shares = summed[7:]
     factor = 1.0 / math.sqrt(token_count * lax.axis_size("fsdp") * lax.axis_size("replica"))

time: 1330 us -> 983 us (0.74)
  blocking collectives: 632 us -> 48 us
  waiting for transfers between devices: 383 us -> 625 us
    psum x1, blocking collectives: 607 us -> 22.7 us  [local(): lax.psum((attention_shares[0], attention_shares[1], attention_shares[2],...]
    psum x0 -> x1, waiting for transfers between devices: none -> 212 us  [local(): lax.psum((attention_shares[0], attention_shares[1], attention_shares[2],...]
    reduce_scatter x1, waiting for transfers between devices: 0.01 us -> 23 us  [local(): lax.psum_scatter(grad_query.astype(jnp.bfloat16), 'fsdp', scatter_dimensi...]
    unnamed x161 -> x167, local copies, waits for them, and re-layouts: 40.2 us -> 37.6 us
  transfers between devices with their start and end apart: 14 -> 15, of which waited for: 9 -> 11; matrix products, arithmetic and copies ran while one was open for 14% -> 19% of each run, Pallas kernels for 0% -> 0%
where the time goes in v1:
time: 983 us; the launch traced here: 974 us
  waiting for transfers between devices  625 us (64%)
  matrix products  163 us (17%)
  other arithmetic  63.8 us (6%)
  local copies, waits for them, and re-layouts  55.9 us (6%)
  blocking collectives  48 us (5%)
  between operations  17 us (2%)
    psum x1, waiting for transfers between devices, local(): lax.psum((attention_shares[0], attention_shares[1], attention_shares[2],...  212 us
    reduce_scatter x1, waiting for transfers between devices, local(): lax.psum_scatter(grad_up.astype(jnp.bfloat16), 'fsdp', scatter_dimension=...  61.1 us
    reduce_scatter x1, waiting for transfers between devices, local(): lax.psum_scatter(grad_gate.astype(jnp.bfloat16), 'fsdp', scatter_dimensio...  60.8 us
    reduce_scatter x1, waiting for transfers between devices, local(): lax.psum_scatter(grad_down.astype(jnp.bfloat16), 'fsdp', scatter_dimensio...  60.8 us
    reduce_scatter x1, waiting for transfers between devices, local(): lax.psum_scatter(grad_out.astype(jnp.bfloat16), 'fsdp', scatter_dimension...  47.2 us
    dot_general x7, matrix products, contract_rows(): lax.dot_general(left, right, (((0,), (0,)), ((), ())), preferred_element_...  41.7 us
    all_gather x1, waiting for transfers between devices, local(): lax.all_gather(down_weight, 'fsdp', axis=0, tiled=True)  38.5 us
    all_gather x1, waiting for transfers between devices, local(): lax.all_gather(up_weight, 'fsdp', axis=0, tiled=True)  38.2 us
  transfers between devices with their start and end apart: 15, of which 11 were waited for; matrix products, arithmetic and copies ran while one was open for 19% of the time, Pallas kernels for 0%

profile of v1, /device:TPU:0, one launch (start us, length us, event | category | flops | bytes accessed | tf_op | source)
XLA Modules:
  0.0 974.0 jit_solution(18263476295955161118)
XLA Ops:
  13.0 6.0 all-gather
  21.1 8.1 all-reduce.11
  30.4 5.1 all-gather.1
  36.7 1.8 fusion.78
  38.6 2.9 fusion.95
  45.0 14.2 %all-gather.10.cloned.1.call-done = bf16[1024,1024]{1,0:T(8,128)(2,1)} async-done(((bf16[256,1024]{1,0:T(8,128)(2,1)}), bf16[1024,1024]{1,0:T(8,128)(2,1)}) %all-gather.10.cloned.1.call-update) | async-done | bytes 2097168 | tf_op jit(solution)/shard_map/all_gather | solution.py:110
  59.2 2.9 convolution_convert_fusion.9
  66.2 1.8 subtract_convert_fusion.1
  67.9 27.4 %all-gather.14.cloned.1.call-done = bf16[1024,2048]{1,0:T(8,128)(2,1)} async-done(((bf16[256,2048]{1,0:T(8,128)(2,1)}), bf16[1024,2048]{1,0:T(8,128)(2,1)}) %all-gather.14.cloned.1.call-update) | async-done | bytes 4194320 | tf_op jit(solution)/shard_map/all_gather | solution.py:108
  95.3 4.9 fusion.93
  105.0 2.0 multiply_multiply_fusion
  107.0 1.7 subtract_convert_fusion
  112.4 5.6 fusion.103
  118.0 8.6 fusion.102
  126.6 3.1 fusion.49
  129.7 1.8 copy-done.9
  134.3 5.5 multiply_reduce_fusion.5
  142.4 36.7 %all-gather.18.cloned.1.call-done = bf16[1024,3072]{1,0:T(8,128)(2,1)} async-done(((bf16[256,3072]{1,0:T(8,128)(2,1)}), bf16[1024,3072]{1,0:T(8,128)(2,1)}) %all-gather.18.cloned.1.call-update) | async-done | bytes 6291472 | tf_op jit(solution)/shard_map/all_gather | solution.py:177
  179.1 9.7 fusion.108
  188.7 38.2 %all-gather.20.cloned.1.call-done = bf16[1024,3072]{1,0:T(8,128)(2,1)} async-done(((bf16[256,3072]{1,0:T(8,128)(2,1)}), bf16[1024,3072]{1,0:T(8,128)(2,1)}) %all-gather.20.cloned.1.call-update) | async-done | bytes 6291472 | tf_op jit(solution)/shard_map/all_gather | solution.py:178
  226.9 9.5 fusion.109
  236.4 38.5 %all-gather.22.cloned.1.call-done = bf16[3072,1024]{1,0:T(8,128)(2,1)} async-done(((bf16[768,1024]{1,0:T(8,128)(2,1)}), bf16[3072,1024]{1,0:T(8,128)(2,1)}) %all-gather.22.cloned.1.call-update) | async-done | bytes 6291472 | tf_op jit(solution)/shard_map/all_gather | solution.py:179
  274.9 11.5 %multiply_convert_fusion = (bf16[512,3072]{1,0:T(8,128)(2,1)S(1)}, bf16[512,3072]{1,0:T(8,128)(2,1)S(1)}, bf16[512,3072]{1,0:T(8,128)(2,1)}) fusion(f32[512,3072]{1,0:T(8,128)} %fusion.108, f32[512,3072]{1,0:T(8,128)} %fusion.109, bf16[3072,1024]{1,0:T(8,128)(2,1)} %all-gather.22.cloned.1.call-done, bf16[512,1024]{1,0:T(8,128)(2,1)} %param.39, ...), kind=kOutput, calls=%fused_computation.10 | convolution fusion | flops 3244818432 | bytes 29362176 | tf_op jit(solution)/shard_map/dot_general | solution.py:69
  286.4 8.3 fusion.110
  294.8 3.8 multiply_reduce_fusion.2
  300.8 2.4 convolution_convert_fusion.5
  304.9 2.3 copy.226
  307.2 8.6 fusion.2
  315.8 2.3 copy.225
  318.0 3.5 fusion.11
  324.4 1.9 copy-done.10
  326.4 4.7 fusion.4
  334.0 2.9 fusion.63
  342.6 2.9 convolution_convert_fusion.7
  346.7 3.0 convolution_bitcast_fusion.1
  349.8 5.6 fusion.34
  356.4 2.8 convolution_convert_fusion.6
  360.7 1.9 multiply_bitcast_fusion.1
  365.6 1.9 fusion.98
  367.4 5.0 copy.222
  372.5 3.8 copy.223
  376.2 4.5 multiply_subtract_fusion
  380.9 3.7 multiply_reduce_fusion
  388.4 7.3 fusion.10
  397.0 4.5 convolution_convert_fusion.4
  403.1 5.9 convolution_convert_fusion.3
  409.0 8.4 convolution_convert_fusion.2
  417.5 8.9 convolution_convert_fusion.1
  426.7 8.4 convolution_convert_fusion
  435.2 23.0 %reduce-scatter.8.cloned.1.call-done = bf16[256,2048]{1,0:T(8,128)(2,1)} async-done(((bf16[1024,2048]{1,0:T(8,128)(2,1)}), bf16[256,2048]{1,0:T(8,128)(2,1)}) %reduce-scatter.8.cloned.1.call-update) | async-done | bytes 1048592 | tf_op jit(solution)/shard_map/reduce_scatter | solution.py:323
  458.2 47.2 %reduce-scatter.14.cloned.1.call-done = bf16[512,1024]{1,0:T(8,128)(2,1)} async-done(((bf16[2048,1024]{1,0:T(8,128)(2,1)}), bf16[512,1024]{1,0:T(8,128)(2,1)}) %reduce-scatter.14.cloned.1.call-update) | async-done | bytes 1048592 | tf_op jit(solution)/shard_map/reduce_scatter | solution.py:338
  505.5 60.8 %reduce-scatter.16.cloned.1.call-done = bf16[256,3072]{1,0:T(8,128)(2,1)} async-done(((bf16[1024,3072]{1,0:T(8,128)(2,1)}), bf16[256,3072]{1,0:T(8,128)(2,1)}) %reduce-scatter.16.cloned.1.call-update) | async-done | bytes 1572880 | tf_op jit(solution)/shard_map/reduce_scatter | solution.py:220
  566.3 61.1 %reduce-scatter.18.cloned.1.call-done = bf16[256,3072]{1,0:T(8,128)(2,1)} async-done(((bf16[1024,3072]{1,0:T(8,128)(2,1)}), bf16[256,3072]{1,0:T(8,128)(2,1)}) %reduce-scatter.18.cloned.1.call-update) | async-done | bytes 1572880 | tf_op jit(solution)/shard_map/reduce_scatter | solution.py:223
  627.3 60.8 %reduce-scatter.20.cloned.1.call-done = bf16[768,1024]{1,0:T(8,128)(2,1)} async-done(((bf16[3072,1024]{1,0:T(8,128)(2,1)}), bf16[768,1024]{1,0:T(8,128)(2,1)}) %reduce-scatter.20.cloned.1.call-update) | async-done | bytes 1572880 | tf_op jit(solution)/shard_map/reduce_scatter | solution.py:226
  689.5 3.3 fusion.111
  695.7 4.2 fusion.28
  699.9 6.1 all-reduce.10
  706.3 22.7 %all-reduce.8 = (bf16[256]{0:T(256)(128)(2,1)S(1)}, bf16[32]{0:T(256)(128)(2,1)S(1)}, bf16[32]{0:T(256)(128)(2,1)S(1)}, bf16[256]{0:T(256)(128)(2,1)S(1)}) all-reduce(bf16[256]{0:T(256)(128)(2,1)S(1)} %dynamic-slice.28, bf16[32]{0:T(256)(128)(2,1)S(1)} %dynamic-slice.30, ...), channel_id=1, replica_groups=mesh['fsdp'=4,'replica'=8] {'replica'}, use_global_device_ids=true, to_apply=%region_19.20 | all-reduce | flops 576 | bytes 2304 | tf_op jit(solution)/shard_map/psum | solution.py:342
  731.2 3.3 fusion.27
  734.5 7.2 add_convert_fusion.1
  741.7 212.5 %all-reduce.14.cloned.1.call-done = (bf16[256,2048]{1,0:T(8,128)(2,1)}, bf16[256,1024]{1,0:T(8,128)(2,1)}, bf16[256,1024]{1,0:T(8,128)(2,1)}, bf16[512,1024]{1,0...) async-done(((bf16[256,2048]{1,0:T(8,128)(2,1)}, bf16[256,1024]{1,0:T(8,128)(2,1)}, bf16[256,1024]{1,0:T(8,128)(2,1)}, ...) | async-done | bytes 7864336 | tf_op jit(solution)/shard_map/psum | solution.py:342
  954.1 3.6 convert_multiply_fusion
  957.8 2.0 convert_multiply_fusion.1
  959.8 2.0 convert_multiply_fusion.2
  (258 shorter events, 70.7 us)
Async XLA Ops:
  7.2 31.4 %all-gather.12.cloned.1.call-start = ((), (), s32[]{:S(2)}) async-start(), calls=%async_computation.8 | async-start | bytes 2621440 | tf_op jit(solution)/shard_map/all_gather | solution.py:109
  7.9 51.3 %all-gather.10.cloned.1.call-start = ((), (), s32[]{:S(2)}) async-start(), calls=%async_computation.7 | async-start | bytes 2621440 | tf_op jit(solution)/shard_map/all_gather | solution.py:110
  8.7 86.6 %all-gather.14.cloned.1.call-start = ((), (), s32[]{:S(2)}) async-start(), calls=%async_computation.9 | async-start | bytes 5242880 | tf_op jit(solution)/shard_map/all_gather | solution.py:108
  9.4 124.9 %all-gather.16.cloned.1.call-start = ((), (), s32[]{:S(2)}) async-start(), calls=%async_computation.10 | async-start | bytes 5242880 | tf_op jit(solution)/shard_map/all_gather | solution.py:113
  10.0 3.0 copy-start.65
  10.0 9.0 copy-start.20
  10.0 169.1 %all-gather.18.cloned.1.call-start = ((), (), s32[]{:S(2)}) async-start(), calls=%async_computation.11 | async-start | bytes 7864320 | tf_op jit(solution)/shard_map/all_gather | solution.py:177
  10.6 8.7 copy-start.59
  10.6 9.9 %copy-start.66 = (bf16[32]{0:T(256)(128)(2,1)S(1)}, bf16[32]{0:T(256)(128)(2,1)}, u32[]{:S(2)}) copy-start(bf16[32]{0:T(256)(128)(2,1)} %param.33) | copy-start | bytes 196
  10.6 10.2 %copy-start.67 = (bf16[32]{0:T(256)(128)(2,1)S(1)}, bf16[32]{0:T(256)(128)(2,1)}, u32[]{:S(2)}) copy-start(bf16[32]{0:T(256)(128)(2,1)} %param.32) | copy-start | bytes 196
  10.6 19.8 %copy-start.68 = (bf16[256]{0:T(256)(128)(2,1)S(1)}, bf16[256]{0:T(256)(128)(2,1)}, u32[]{:S(2)}) copy-start(bf16[256]{0:T(256)(128)(2,1)} %param.35) | copy-start | bytes 1540
  10.6 216.3 %all-gather.20.cloned.1.call-start = ((), (), s32[]{:S(2)}) async-start(), calls=%async_computation.12 | async-start | bytes 7864320 | tf_op jit(solution)/shard_map/all_gather | solution.py:178
  11.2 263.7 %all-gather.22.cloned.1.call-start = ((), (), s32[]{:S(2)}) async-start(), calls=%async_computation.13 | async-start | bytes 7864320 | tf_op jit(solution)/shard_map/all_gather | solution.py:179
  12.0 423.2 %reduce-scatter.10.cloned.1.call-start = ((), (), s32[]{:S(2)}) async-start(), calls=%async_computation.15 | async-start | bytes 2621440 | tf_op jit(solution)/shard_map/reduce_scatter | solution.py:326
  19.0 40.3 %copy-start.48 = (f32[4,1,256]{2,1,0:T(1,128)}, f32[4,1,256]{2,1,0:T(1,128)S(1)}, u32[]{:S(2)}) copy-start(f32[4,1,256]{2,1,0:T(1,128)S(1)} %convert_element_type.211) | copy-start | bytes 12292
  19.3 40.0 %copy-start.51 = (f32[512]{0:T(512)}, f32[512]{0:T(512)S(1)}, u32[]{:S(2)}) copy-start(f32[512]{0:T(512)S(1)} %add_rsqrt_fusion.3) | copy-start | bytes 6148
  29.7 9.0 copy-start.56
  62.1 2.2 copy-start.44
  62.1 3.1 copy-start.57
  102.2 2.7 copy-start.54
  126.6 4.9 copy-start.9
  126.6 5.1 copy-start.37
  126.6 5.1 copy-start.47
  134.3 6.9 copy-start.45
  188.7 86.1 %copy-start.53 = (f32[512]{0:T(512)S(1)}, f32[512]{0:T(512)}, u32[]{:S(2)}) copy-start(f32[512]{0:T(512)} %compare_convert_fusion) | copy-start | bytes 6148
  286.4 8.3 copy-start.72
  286.4 8.3 copy-start.71
  286.4 8.3 copy-start.12
  286.4 8.3 copy-start.61
  294.7 3.8 copy-start.33
  298.6 2.2 copy-start.63
  300.7 2.4 copy-start.14
  315.8 2.3 copy-start.46
  318.0 3.9 copy-start.19
  321.9 4.5 copy-start.10
  326.4 4.7 copy-start.38
  337.8 2.3 copy-start.16
  337.8 2.3 copy-start.50
  340.1 2.5 copy-start.21
  340.2 2.5 copy-start.49
  340.2 2.5 copy-start.52
  345.5 4.2 copy-start.39
  345.5 89.6 %reduce-scatter.12.cloned.1.call-start = ((), (), s32[]{:S(2)}) async-start(), calls=%async_computation.16 | async-start | bytes 2621440 | tf_op jit(solution)/shard_map/reduce_scatter | solution.py:329
  349.8 6.6 copy-start.22
  359.1 99.1 %reduce-scatter.8.cloned.1.call-start = ((), (), s32[]{:S(2)}) async-start(), calls=%async_computation.14 | async-start | bytes 5242880 | tf_op jit(solution)/shard_map/reduce_scatter | solution.py:323
  360.7 2.6 copy-start.3
  360.7 3.0 copy-start.8
  372.5 3.8 copy-start.26
  376.2 4.7 copy-start.1
  376.2 4.7 copy-start.18
  385.8 2.6 copy-start.7
  388.4 8.6 copy-start.23
  401.5 103.9 %reduce-scatter.14.cloned.1.call-start = ((), (), s32[]{:S(2)}) async-start(), calls=%async_computation.17 | async-start | bytes 5242880 | tf_op jit(solution)/shard_map/reduce_scatter | solution.py:338
  409.0 157.3 %reduce-scatter.16.cloned.1.call-start = ((), (), s32[]{:S(2)}) async-start(), calls=%async_computation.18 | async-start | bytes 7864320 | tf_op jit(solution)/shard_map/reduce_scatter | solution.py:220
  417.5 209.9 %reduce-scatter.18.cloned.1.call-start = ((), (), s32[]{:S(2)}) async-start(), calls=%async_computation.19 | async-start | bytes 7864320 | tf_op jit(solution)/shard_map/reduce_scatter | solution.py:223
  426.5 261.6 %reduce-scatter.20.cloned.1.call-start = ((), (), s32[]{:S(2)}) async-start(), calls=%async_computation.20 | async-start | bytes 7864320 | tf_op jit(solution)/shard_map/reduce_scatter | solution.py:226
  435.1 519.0 %all-reduce.14.cloned.1.call-start = ((), (), s32[]{:S(2)}) async-start(), calls=%async_computation.21 | async-start | bytes 15728640 | tf_op jit(solution)/shard_map/psum | solution.py:342
  689.5 3.4 copy-start.64
  689.5 3.4 copy-start.70
  692.9 2.8 copy-start.62
  731.2 3.3 copy-start.13
  731.2 3.3 copy-start.73
  954.1 3.6 copy-start.32
  963.4 2.7 copy-start.42
  (25 other events, 37.4 us)
Sparse Core Ops, SparseCore 0:
  9.6 25.4 all-gather.11
  36.6 22.5 all-gather.9
  60.8 34.4 all-gather.13
  96.7 34.4 all-gather.15
  132.6 46.3 all-gather.17
  180.5 46.3 all-gather.19
  228.5 46.3 all-gather.21
  345.7 31.4 reduce-scatter.9
  379.8 31.4 reduce-scatter.11
  413.7 44.4 reduce-scatter.7
  460.9 44.5 reduce-scatter.13
  507.9 58.3 reduce-scatter.15
  569.0 58.3 reduce-scatter.17
  629.7 58.3 reduce-scatter.19
  694.3 259.8 all-reduce.13

commit v2 on v0

--- a/solution.py
+++ b/solution.py
@@ -69,6 +69,40 @@
     return lax.dot_general(
         left, right, (((1,), (1,)), ((), ())), preferred_element_type=jnp.float32
     )
+
+
+def partner(bit):
+    return [(i, i ^ bit) for i in range(lax.axis_size("fsdp"))]
+
+
+def split_columns(left, core):
+    rows, width = left.shape
+    parts = left.reshape(rows, 2, 2, width // 4)
+    here = lax.dynamic_index_in_dim(parts, core, 2, keepdims=False)
+    there = lax.dynamic_index_in_dim(parts, 1 - core, 2, keepdims=False)
+    return here.reshape(rows, width // 2), there.reshape(rows, width // 2)
+
+
+def start_shares(left, right):
+    core = lax.axis_index("fsdp") % 2
+    here, there = split_columns(left, core)
+    sent = contract_rows(there, right).astype(jnp.bfloat16)
+    return here, right, sent
+
+
+def chip_shares(started):
+    here, right, sent = started
+    received = lax.ppermute(sent, "fsdp", partner(1))
+    return (contract_rows(here, right) + received.astype(jnp.float32)).astype(jnp.bfloat16)
+
+
+def finish_shares(half):
+    side = lax.axis_index("fsdp") // 2
+    half = half.reshape(2, half.shape[0] // 2, half.shape[1])
+    kept = lax.dynamic_index_in_dim(half, side, 0, keepdims=False)
+    sent = lax.dynamic_index_in_dim(half, 1 - side, 0, keepdims=False)
+    received = lax.ppermute(sent, "fsdp", partner(2))
+    return (kept.astype(jnp.float32) + received.astype(jnp.float32)).astype(jnp.bfloat16)
 
 
 def masked_scores(query_rows, key_rows, seg_rows, seg_keys, first):
@@ -199,33 +233,19 @@
     )
     gate_back, up_back, down_back = (feed_back[1], feed_back[2], feed_back[3])
     grad_result_low = grad_result.astype(jnp.bfloat16)
-    grad_down = contract_rows(activation_low, grad_result_low)
+    grad_down = start_shares(activation_low, grad_result_low)
     grad_act = product_with_transpose(grad_result_low, down_back)
     grad_silu = grad_act * up_value
     gate_grad_low = (grad_silu * (sigma + gate * sigma * (1.0 - sigma))).astype(jnp.bfloat16)
     up_grad_low = (grad_act * silu_value).astype(jnp.bfloat16)
-    grad_gate = contract_rows(hidden_second, gate_grad_low)
-    grad_up = contract_rows(hidden_second, up_grad_low)
+    grad_gate = start_shares(hidden_second, gate_grad_low)
+    grad_up = start_shares(hidden_second, up_grad_low)
     grad_hidden_second = product_with_transpose(gate_grad_low, gate_back) + product_with_transpose(
         up_grad_low, up_back
     )
     grad_second_gain = jnp.sum(grad_hidden_second * unit_second, axis=0)
     grad_middle = grad_result + norm_back(
         grad_hidden_second, unit_second, inverse_second, second_gain
-    )
-    feed_shares = (
-        lax.psum_scatter(
-            grad_second_gain.astype(jnp.bfloat16), "fsdp", scatter_dimension=0, tiled=True
-        ).astype(jnp.float32),
-        lax.psum_scatter(
-            grad_gate.astype(jnp.bfloat16), "fsdp", scatter_dimension=0, tiled=True
-        ).astype(jnp.float32),
-        lax.psum_scatter(
-            grad_up.astype(jnp.bfloat16), "fsdp", scatter_dimension=0, tiled=True
-        ).astype(jnp.float32),
-        lax.psum_scatter(
-            grad_down.astype(jnp.bfloat16), "fsdp", scatter_dimension=0, tiled=True
-        ).astype(jnp.float32),
     )
     attention_back = (
         lax.all_gather(attention_gain, "fsdp", axis=0, tiled=True),
@@ -243,7 +263,10 @@
         attention_back[6],
     )
     middle_reduced = grad_middle.astype(jnp.bfloat16)
-    grad_out = contract_rows(mixed_low, middle_reduced)
+    middle_reduced, grad_down, grad_gate, grad_up = lax.optimization_barrier(
+        (middle_reduced, grad_down, grad_gate, grad_up)
+    )
+    grad_out = start_shares(mixed_low, middle_reduced)
     grad_mixed_low = (
         product_with_transpose(middle_reduced, output_backward)
         .astype(jnp.bfloat16)
@@ -288,6 +311,15 @@
             )
             / math.sqrt(HEAD_SIZE)
         )
+    query_grads, key_gradient_total, value_gradient_total, feed_halves = lax.optimization_barrier(
+        (
+            query_grads,
+            key_gradient_total,
+            value_gradient_total,
+            (chip_shares(grad_gate), chip_shares(grad_up), chip_shares(grad_down)),
+        )
+    )
+    feed_summed = lax.psum(tuple(finish_shares(half) for half in feed_halves), "replica")
     grad_query_rot = jnp.concatenate(query_grads, axis=0).reshape(
         token_count, QUERY_HEADS, HEAD_SIZE
     )
@@ -306,9 +338,9 @@
     value_gradient_reduced = value_gradient_total.astype(jnp.bfloat16).reshape(
         token_count, KEY_VALUE_HEADS * HEAD_SIZE
     )
-    grad_query = contract_rows(hidden_state, query_grad_low)
-    grad_key = contract_rows(hidden_state, key_gradient_reduced)
-    grad_value = contract_rows(hidden_state, value_gradient_reduced)
+    grad_value = start_shares(hidden_state, value_gradient_reduced)
+    grad_query = start_shares(hidden_state, query_grad_low)
+    grad_key = start_shares(hidden_state, key_gradient_reduced)
     grad_hidden = (
         product_with_transpose(query_grad_low, query_back)
         + product_with_transpose(key_gradient_reduced, key_back)
@@ -317,61 +349,42 @@
     grad_first_gain = jnp.sum(grad_hidden * unit_first, axis=0)
     grad_inputs = grad_middle + norm_back(grad_hidden, unit_first, inverse_first, first_gain)
     attention_shares = (
-        lax.psum_scatter(
-            grad_first_gain.astype(jnp.bfloat16), "fsdp", scatter_dimension=0, tiled=True
-        ).astype(jnp.float32),
-        lax.psum_scatter(
-            grad_query.astype(jnp.bfloat16), "fsdp", scatter_dimension=0, tiled=True
-        ).astype(jnp.float32),
-        lax.psum_scatter(
-            grad_key.astype(jnp.bfloat16), "fsdp", scatter_dimension=0, tiled=True
-        ).astype(jnp.float32),
-        lax.psum_scatter(
-            grad_value.astype(jnp.bfloat16), "fsdp", scatter_dimension=0, tiled=True
-        ).astype(jnp.float32),
-        lax.psum_scatter(
-            grad_query_scale.astype(jnp.bfloat16), "fsdp", scatter_dimension=0, tiled=True
-        ).astype(jnp.float32),
-        lax.psum_scatter(
-            grad_key_scale.astype(jnp.bfloat16), "fsdp", scatter_dimension=0, tiled=True
-        ).astype(jnp.float32),
-        lax.psum_scatter(
-            grad_out.astype(jnp.bfloat16), "fsdp", scatter_dimension=0, tiled=True
-        ).astype(jnp.float32),
-    )
-    summed = lax.psum(
-        (
-            attention_shares[0],
-            attention_shares[1],
-            attention_shares[2],
-            attention_shares[3],
-            attention_shares[4],
-            attention_shares[5],
-            attention_shares[6],
-            feed_shares[0],
-            feed_shares[1],
-            feed_shares[2],
-            feed_shares[3],
-        ),
-        "replica",
-    )
-    attention_shares = summed[:7]
-    feed_shares = summed[7:]
+        finish_shares(chip_shares(grad_query)),
+        finish_shares(chip_shares(grad_key)),
+        finish_shares(chip_shares(grad_value)),
+        finish_shares(chip_shares(grad_out)),
+    )
+    attention_shares, feed_summed = lax.optimization_barrier((attention_shares, feed_summed))
+    attention_summed = lax.psum(attention_shares, "replica")
+    gains = lax.psum(
+        jnp.concatenate([grad_first_gain, grad_second_gain, grad_query_scale, grad_key_scale]),
+        ("fsdp", "replica"),
+    )
+    place = lax.axis_index("fsdp")
+    groups = lax.axis_size("fsdp")
+    gain_shares = []
+    begin = 0
+    for grad in (grad_first_gain, grad_second_gain, grad_query_scale, grad_key_scale):
+        length = grad.shape[0] // groups
+        gain_shares.append(lax.dynamic_slice(gains, (begin + place * length,), (length,)))
+        begin += grad.shape[0]
+    first_share, second_share, query_share, key_share = gain_shares
+    wide = [share.astype(jnp.float32) for share in attention_summed + feed_summed]
     factor = 1.0 / math.sqrt(token_count * lax.axis_size("fsdp") * lax.axis_size("replica"))
     return (
         output,
         grad_inputs.astype(jnp.bfloat16),
-        attention_shares[0] * factor,
-        attention_shares[1] * factor,
-        attention_shares[2] * factor,
-        attention_shares[3] * factor,
-        attention_shares[4] * factor,
-        attention_shares[5] * factor,
-        attention_shares[6] * factor,
-        feed_shares[0] * factor,
-        feed_shares[1] * factor,
-        feed_shares[2] * factor,
-        feed_shares[3] * factor,
+        first_share * factor,
+        wide[0] * factor,
+        wide[1] * factor,
+        wide[2] * factor,
+        query_share * factor,
+        key_share * factor,
+        wide[3] * factor,
+        second_share * factor,
+        wide[4] * factor,
+        wide[5] * factor,
+        wide[6] * factor,
     )
 
 

time: 1330 us -> 867 us (0.65)
  blocking collectives: 632 us -> 62.3 us
  waiting for transfers between devices: 383 us -> 432 us
  local copies, waits for them, and re-layouts: 58.3 us -> 104 us
  other arithmetic: 64.1 us -> 83.1 us
    psum x1, blocking collectives: 607 us -> 43.1 us  [local(): lax.psum(jnp.concatenate([grad_first_gain, grad_second_gain, grad_query_s...]
    reduce_scatter x7 -> x0, waiting for transfers between devices: 223 us -> none  [the longest x1 61.1 us: local(): lax.psum_scatter(grad_up.astype(jnp.bfloat16), 'fsdp', scatter_dimension=...]
    psum x0 -> x2, waiting for transfers between devices: none -> 165 us  [the longest x1 92.7 us: local(): lax.psum(tuple((finish_shares(half) for half in feed_halves)), 'replica')]
    ppermute x0 -> x14, waiting for transfers between devices: none -> 128 us  [the longest x7 128 us: finish_shares(): received = lax.ppermute(sent, 'fsdp', partner(2))]
    convert_element_type x4 -> x11, other arithmetic: 0.3 us -> 19.8 us  [the longest x7 14.8 us: finish_shares(): (kept.astype(jnp.float32) + received.astype(jnp.float32)).astype(jnp.bflo...]
    dynamic_slice x0 -> x4, local copies, waits for them, and re-layouts: none -> 17.1 us  [split_columns(): there = lax.dynamic_index_in_dim(parts, 1 - core, 2, keepdims=False)]
    unnamed x161 -> x247, local copies, waits for them, and re-layouts: 40.2 us -> 56.5 us
    all_gather x1, waiting for transfers between devices: 14.2 us -> 0.01 us  [local(): lax.all_gather(value_matrix, 'fsdp', axis=0, tiled=True)]
  transfers between devices with their start and end apart: 14 -> 23, of which waited for: 9 -> 14; matrix products, arithmetic and copies ran while one was open for 14% -> 24% of each run, Pallas kernels for 0% -> 0%
where the time goes in v2:
time: 867 us; the launch traced here: 859 us
  waiting for transfers between devices  432 us (50%)
  matrix products  154 us (18%)
  local copies, waits for them, and re-layouts  104 us (12%)
  other arithmetic  83.1 us (10%)
  blocking collectives  62.3 us (7%)
  between operations  16 us (2%)
    ppermute x7, waiting for transfers between devices, finish_shares(): received = lax.ppermute(sent, 'fsdp', partner(2))  128 us
    psum x1, waiting for transfers between devices, local(): lax.psum(tuple((finish_shares(half) for half in feed_halves)), 'replica')  92.7 us
    psum x1, waiting for transfers between devices, local(): attention_summed = lax.psum(attention_shares, 'replica')  72.4 us
    unnamed x247, local copies, waits for them, and re-layouts  56.5 us
    dot_general x14, matrix products, contract_rows(): lax.dot_general(left, right, (((0,), (0,)), ((), ())), preferred_element_...  44.6 us
    psum x1, blocking collectives, local(): lax.psum(jnp.concatenate([grad_first_gain, grad_second_gain, grad_query_s...  43.1 us
    all_gather x1, waiting for transfers between devices, local(): lax.all_gather(down_weight, 'fsdp', axis=0, tiled=True)  40 us
    all_gather x1, waiting for transfers between devices, local(): lax.all_gather(up_weight, 'fsdp', axis=0, tiled=True)  39.8 us
  transfers between devices with their start and end apart: 23, of which 14 were waited for; matrix products, arithmetic and copies ran while one was open for 24% of the time, Pallas kernels for 0%

profile of v2, /device:TPU:0, one launch (start us, length us, event | category | flops | bytes accessed | tf_op | source)
XLA Modules:
  0.0 858.8 jit_solution(16970076880133740728)
XLA Ops:
  12.9 6.0 all-gather
  21.0 8.1 all-reduce.6
  29.9 5.1 all-gather.1
  38.0 3.1 constant_dynamic-slice_fusion.2
  41.2 3.5 copy.289
  52.1 2.9 convolution_convert_fusion.6
  56.3 2.9 all-gather.12.cloned.1.call-done
  59.2 3.2 fusion.97
  71.2 24.1 %all-gather.14.cloned.1.call-done = bf16[1024,2048]{1,0:T(8,128)(2,1)} async-done(((bf16[256,2048]{1,0:T(8,128)(2,1)}), bf16[1024,2048]{1,0:T(8,128)(2,1)}) %all-gather.14.cloned.1.call-update) | async-done | bytes 4194320 | tf_op jit(solution)/shard_map/all_gather | solution.py:142
  95.3 4.8 fusion.98
  112.3 4.8 fusion.92
  117.1 7.7 fusion.91
  124.8 3.1 convolution_bitcast_fusion
  131.2 4.6 multiply_reduce_fusion.5
  140.8 3.5 constant_dynamic-slice_fusion.4
  144.3 3.6 copy.284
  151.6 27.5 %all-gather.18.cloned.1.call-done = bf16[1024,3072]{1,0:T(8,128)(2,1)} async-done(((bf16[256,3072]{1,0:T(8,128)(2,1)}), bf16[1024,3072]{1,0:T(8,128)(2,1)}) %all-gather.18.cloned.1.call-update) | async-done | bytes 6291472 | tf_op jit(solution)/shard_map/all_gather | solution.py:211
  179.1 8.0 fusion.99
  187.1 39.8 %all-gather.20.cloned.1.call-done = bf16[1024,3072]{1,0:T(8,128)(2,1)} async-done(((bf16[256,3072]{1,0:T(8,128)(2,1)}), bf16[1024,3072]{1,0:T(8,128)(2,1)}) %all-gather.20.cloned.1.call-update) | async-done | bytes 6291472 | tf_op jit(solution)/shard_map/all_gather | solution.py:212
  226.9 8.0 fusion.100
  234.9 40.0 %all-gather.22.cloned.1.call-done = bf16[3072,1024]{1,0:T(8,128)(2,1)} async-done(((bf16[768,1024]{1,0:T(8,128)(2,1)}), bf16[3072,1024]{1,0:T(8,128)(2,1)}) %all-gather.22.cloned.1.call-update) | async-done | bytes 6291472 | tf_op jit(solution)/shard_map/all_gather | solution.py:213
  274.9 11.5 %multiply_convert_fusion = (bf16[512,3072]{1,0:T(8,128)(2,1)S(1)}, bf16[512,3072]{1,0:T(8,128)(2,1)S(1)}, bf16[512,3072]{1,0:T(8,128)(2,1)}) fusion(f32[512,3072]{1,0:T(8,128)} %fusion.99, f32[512,3072]{1,0:T(8,128)} %fusion.100, bf16[512,1024]{1,0:T(8,128)(2,1)S(1)} %copy-done.56, bf16[3072,1024]{1,0:T(8,128)(2,1)} %all-gather.22.cloned.1.call-done), kind=kOutput, calls=%fused_computation.13 | convolution fusion | flops 3243245568 | bytes 29360128 | tf_op jit(solution)/shard_map/dot_general | solution.py:69
  286.5 3.5 convolution_convert_fusion.1
  289.9 3.4 convolution_convert_fusion
  293.4 3.4 fusion.101
  296.9 5.6 multiply_reduce_fusion.2
  302.5 7.5 reshape.548
  310.0 9.1 %constant_dynamic-slice_fusion.6 = (bf16[512,2,1,768]{3,2,1,0:T(2,128)(2,1)}, bf16[512,2,1,768]{3,2,1,0:T(2,128)(2,1)}) fusion(bf16[512,2,2,768]{3,2,1,0:T(2,128)(2,1)S(1)} %reshape.548, s32[]{:T(128)S(6)} %select_n.120, s32[]{:T(128)S(6)} %select_n.119), kind=kLoop, calls=%fused_computation.195 | loop fusion | bytes 6291464 | tf_op jit(solution)/shard_map/jit(dynamic_index_in_dim)/dynamic_slice | solution.py:82
  319.0 8.3 copy.282
  327.3 6.2 copy.283
  333.5 5.4 convolution_convert_fusion.2
  347.7 5.5 fusion.11
  356.3 5.4 fusion.2
  362.6 2.7 convolution_convert_fusion.5
  365.5 4.8 fusion.4
  370.5 4.4 add_convert_fusion.8
  386.7 4.3 add_convert_fusion.3
  391.0 5.5 add_convert_fusion.2
  396.6 5.5 add_convert_fusion.1
  402.1 5.8 add_convert_fusion
  410.2 4.9 copy.287
  415.1 3.9 copy.286
  419.0 5.0 multiply_subtract_fusion.1
  424.0 3.3 multiply_subtract_fusion
  427.4 3.7 multiply_reduce_fusion
  441.5 7.3 fusion.10
  448.9 2.8 fusion.65
  451.7 2.6 convolution_convert_fusion.4
  454.6 15.4 %collective-permute-done.11 = bf16[256,3072]{1,0:T(8,128)(2,1)} collective-permute-done((bf16[256,3072]{1,0:T(8,128)(2,1)}, bf16[256,3072]{1,0:T(8,128)(2,1)}, u32[]{:S(2)}, u32[]{:S(2)}) %collective-permute-start.11) | collective-permute-done | bytes 1572896 | tf_op jit(solution)/shard_map/ppermute | solution.py:104
  470.0 3.6 fusion.20
  473.6 30.1 %collective-permute-done.12 = bf16[256,3072]{1,0:T(8,128)(2,1)} collective-permute-done((bf16[256,3072]{1,0:T(8,128)(2,1)}, bf16[256,3072]{1,0:T(8,128)(2,1)}, u32[]{:S(2)}, u32[]{:S(2)}) %collective-permute-start.12) | collective-permute-done | bytes 1572896 | tf_op jit(solution)/shard_map/ppermute | solution.py:104
  503.7 3.1 fusion.19
  506.9 29.9 %collective-permute-done.13 = bf16[768,1024]{1,0:T(8,128)(2,1)} collective-permute-done((bf16[768,1024]{1,0:T(8,128)(2,1)}, bf16[768,1024]{1,0:T(8,128)(2,1)}, u32[]{:S(2)}, u32[]{:S(2)}) %collective-permute-start.13) | collective-permute-done | bytes 1572896 | tf_op jit(solution)/shard_map/ppermute | solution.py:104
  536.8 3.2 fusion.18
  554.8 2.9 add_convert_fusion.4
  560.8 11.1 %collective-permute-done.10 = bf16[512,1024]{1,0:T(8,128)(2,1)S(1)} collective-permute-done((bf16[512,1024]{1,0:T(8,128)(2,1)S(1)}, bf16[512,1024]{1,0:T(8,128)(2,1)S(1)}, u32[]{:S(2)}, u32[]{:S(2)}) %collective-permute-start.10) | collective-permute-done | bytes 1048608 | tf_op jit(solution)/shard_map/ppermute | solution.py:104
  573.3 9.8 %collective-permute-done.6 = bf16[256,1024]{1,0:T(8,128)(2,1)S(1)} collective-permute-done((bf16[256,1024]{1,0:T(8,128)(2,1)S(1)}, bf16[256,1024]{1,0:T(8,128)(2,1)S(1)}, u32[]{:S(2)}, u32[]{:S(2)}) %collective-permute-start.6) | collective-permute-done | bytes 524320 | tf_op jit(solution)/shard_map/ppermute | solution.py:104
  584.1 31.4 %collective-permute-done.8 = bf16[256,1024]{1,0:T(8,128)(2,1)S(1)} collective-permute-done((bf16[256,1024]{1,0:T(8,128)(2,1)S(1)}, bf16[256,1024]{1,0:T(8,128)(2,1)S(1)}, u32[]{:S(2)}, u32[]{:S(2)}) %collective-permute-start.8) | collective-permute-done | bytes 524320 | tf_op jit(solution)/shard_map/ppermute | solution.py:104
  617.9 92.7 %all-reduce.12.cloned.1.call-done = (bf16[256,3072]{1,0:T(8,128)(2,1)}, bf16[256,3072]{1,0:T(8,128)(2,1)}, bf16[768,1024]{1,0:T(8,128)(2,1)}) async-done(((bf16[256,3072]{1,0:T(8,128)(2,1)}, bf16[256,3072]{1,0:T(8,128)(2,1)}, bf16[768,1024]{1,0:T(8,128)(2,1)}), (bf16[256,3072]{1,0:T(8,128)(2,1)}, bf16[256,3072]{1,0:T(8,128)(2,1)}, bf16[768,1024]{1,0:T(8,128)(2,1)})) %all-reduce.12.cloned.1.call-update) | async-done | bytes 4718608 | tf_op jit(solution)/shard_map/psum | solution.py:322
  710.7 8.5 fusion.31
  719.2 43.1 %psum.56 = f32[2304]{0:T(1024)S(1)} all-reduce(f32[2304]{0:T(1024)S(1)} %pad_maximum_fusion.4), channel_id=1, replica_groups=mesh['fsdp'=4,'replica'=8] {'fsdp','replica'}, use_global_device_ids=true, to_apply=%region_23.24 | all-reduce | flops 2304 | bytes 18432 | tf_op jit(solution)/shard_map/psum | solution.py:359
  763.6 3.3 fusion.30
  773.0 72.4 %all-reduce.10.cloned.1.call-done = (bf16[256,2048]{1,0:T(8,128)(2,1)}, bf16[256,1024]{1,0:T(8,128)(2,1)}, bf16[256,1024]{1,0:T(8,128)(2,1)}, bf16[512,1024]{1,0:T(8,128)(2,1)}) async-done(((bf16[256,2048]{1,0:T(8,128)(2,1)}, bf16[256,1024]{1,0:T(8,128)(2,1)}, bf16[256,1024]{1,0:T(8,128)(2,1)}, bf16[512,1024]{1,0:T(8,128)(2,1)}), (bf16[256,2048]{1,0:T(8,128)(2,1)}, bf16[256,1024]{1,0:T(8,128)(2,1)}, ...) | async-done | bytes 3145744 | tf_op jit(solution)/shard_map/psum | solution.py:358
  845.4 2.9 convert_multiply_fusion.6
  (380 shorter events, 124.0 us)
Async XLA Ops:
  7.2 45.0 %all-gather.10.cloned.1.call-start = ((), (), s32[]{:S(2)}) async-start(), calls=%async_computation | async-start | bytes 2621440 | tf_op jit(solution)/shard_map/all_gather | solution.py:144
  7.9 51.3 %all-gather.12.cloned.1.call-start = ((), (), s32[]{:S(2)}) async-start(), calls=%async_computation.1 | async-start | bytes 2621440 | tf_op jit(solution)/shard_map/all_gather | solution.py:143
  8.7 86.6 %all-gather.14.cloned.1.call-start = ((), (), s32[]{:S(2)}) async-start(), calls=%async_computation.2 | async-start | bytes 5242880 | tf_op jit(solution)/shard_map/all_gather | solution.py:142
  9.4 121.8 %all-gather.16.cloned.1.call-start = ((), (), s32[]{:S(2)}) async-start(), calls=%async_computation.3 | async-start | bytes 5242880 | tf_op jit(solution)/shard_map/all_gather | solution.py:147
  10.0 9.0 %copy-start.8 = (bf16[512,1024]{1,0:T(8,128)(2,1)S(1)}, bf16[512,1024]{1,0:T(8,128)(2,1)}, u32[]{:S(2)}) copy-start(bf16[512,1024]{1,0:T(8,128)(2,1)} %param.26) | copy-start | bytes 3145732
  10.0 169.1 %all-gather.18.cloned.1.call-start = ((), (), s32[]{:S(2)}) async-start(), calls=%async_computation.4 | async-start | bytes 7864320 | tf_op jit(solution)/shard_map/all_gather | solution.py:211
  10.6 8.7 %copy-start.99 = (u32[32]{0:T(128)S(1)}, u32[32]{0:T(128)}, u32[]{:S(2)}) copy-start(u32[32]{0:T(128)} %constant.339) | copy-start | bytes 388
  10.6 9.9 %copy-start.95 = (bf16[32]{0:T(256)(128)(2,1)S(1)}, bf16[32]{0:T(256)(128)(2,1)}, u32[]{:S(2)}) copy-start(bf16[32]{0:T(256)(128)(2,1)} %param.32) | copy-start | bytes 196
  10.6 10.2 %copy-start.96 = (bf16[32]{0:T(256)(128)(2,1)S(1)}, bf16[32]{0:T(256)(128)(2,1)}, u32[]{:S(2)}) copy-start(bf16[32]{0:T(256)(128)(2,1)} %param.33) | copy-start | bytes 196
  10.6 19.3 %copy-start.97 = (bf16[256]{0:T(256)(128)(2,1)S(1)}, bf16[256]{0:T(256)(128)(2,1)}, u32[]{:S(2)}) copy-start(bf16[256]{0:T(256)(128)(2,1)} %param.35) | copy-start | bytes 1540
  10.6 216.3 %all-gather.20.cloned.1.call-start = ((), (), s32[]{:S(2)}) async-start(), calls=%async_computation.5 | async-start | bytes 7864320 | tf_op jit(solution)/shard_map/all_gather | solution.py:212
  11.2 263.7 %all-gather.22.cloned.1.call-start = ((), (), s32[]{:S(2)}) async-start(), calls=%async_computation.6 | async-start | bytes 7864320 | tf_op jit(solution)/shard_map/all_gather | solution.py:213
  12.0 698.6 %all-reduce.12.cloned.1.call-start = ((), (), s32[]{:S(2)}) async-start(), calls=%async_computation.8 | async-start | bytes 9437184 | tf_op jit(solution)/shard_map/psum | solution.py:322
  12.9 36.7 %copy-start.81 = (f32[512]{0:T(512)}, f32[512]{0:T(512)S(1)}, u32[]{:S(2)}) copy-start(f32[512]{0:T(512)S(1)} %compare_convert_fusion) | copy-start | bytes 6148
  19.0 17.8 %copy-start.75 = (f32[4,1,256]{2,1,0:T(1,128)}, f32[4,1,256]{2,1,0:T(1,128)S(1)}, u32[]{:S(2)}) copy-start(f32[4,1,256]{2,1,0:T(1,128)S(1)} %convert_element_type.362) | copy-start | bytes 12292
  19.2 17.5 %copy-start.79 = (f32[512]{0:T(512)}, f32[512]{0:T(512)S(1)}, u32[]{:S(2)}) copy-start(f32[512]{0:T(512)S(1)} %add_rsqrt_fusion.3) | copy-start | bytes 6148
  29.1 8.8 %copy-start.84 = (f32[128]{0:T(128)}, f32[128]{0:T(128)S(1)}, u32[]{:S(2)}) copy-start(f32[128]{0:T(128)S(1)} %convert_element_type.276) | copy-start | bytes 1540
  29.2 8.7 %copy-start.87 = (f32[128]{0:T(128)}, f32[128]{0:T(128)S(1)}, u32[]{:S(2)}) copy-start(f32[128]{0:T(128)S(1)} %convert_element_type.274) | copy-start | bytes 1540
  44.7 7.5 copy-start.28
  49.6 57.3 %copy-start.22 = (f32[512,64]{1,0:T(8,128)}, f32[512,64]{1,0:T(8,128)S(1)}, u32[]{:S(2)}) copy-start(f32[512,64]{1,0:T(8,128)S(1)} %get-tuple-element.181) | copy-start | bytes 393220
  62.4 6.4 copy-start.2
  71.2 46.0 %copy-start.10 = (bf16[512,8,64]{2,0,1:T(8,128)(2,1)}, bf16[512,8,64]{2,0,1:T(8,128)(2,1)S(1)}, u32[]{:S(2)}) copy-start(bf16[512,8,64]{2,0,1:T(8,128)(2,1)S(1)} %get-tuple-element.165) | copy-start | bytes 1572868
  71.2 46.0 %copy-start.12 = (bf16[512,8,64]{2,0,1:T(8,128)(2,1)}, bf16[512,8,64]{2,0,1:T(8,128)(2,1)S(1)}, u32[]{:S(2)}) copy-start(bf16[512,8,64]{2,0,1:T(8,128)(2,1)S(1)} %get-tuple-element.166) | copy-start | bytes 1572868
  131.2 6.0 copy-start.77
  150.1 28.9 %copy-start.32 = (bf16[512,1024]{1,0:T(8,128)(2,1)S(1)}, bf16[512,1024]{1,0:T(8,128)(2,1)}, u32[]{:S(2)}) copy-start(bf16[512,1024]{1,0:T(8,128)(2,1)} %multiply_convert_fusion.3) | copy-start | bytes 3145732
  187.1 87.9 %copy-start.56 = (bf16[512,1024]{1,0:T(8,128)(2,1)S(1)}, bf16[512,1024]{1,0:T(8,128)(2,1)}, u32[]{:S(2)}) copy-start(bf16[512,1024]{1,0:T(8,128)(2,1)} %fusion.39) | copy-start | bytes 3145732
  234.9 51.5 %copy-start.70 = (bf16[512,2,1,256]{0,3,1,2:T(8,128)(2,1)S(1)}, bf16[512,2,1,256]{0,3,1,2:T(8,128)(2,1)}, u32[]{:S(2)}) copy-start(bf16[512,2,1,256]{0,3,1,2:T(8,128)(2,1)} %copy.285) | copy-start | bytes 1572868
  286.4 6.9 copy-start.102
  286.4 10.4 %copy-start.100 = (bf16[512,3072]{1,0:T(8,128)(2,1)}, bf16[512,3072]{1,0:T(8,128)(2,1)S(1)}, u32[]{:S(2)}) copy-start(bf16[512,3072]{1,0:T(8,128)(2,1)S(1)} %get-tuple-element.106) | copy-start | bytes 9437188
  286.5 6.9 slice-start.4
  289.9 6.9 slice-start.6
  319.0 8.3 copy-start.7
  356.3 6.3 copy-start.54
  356.3 6.3 copy-start.64
  361.7 29.3 %collective-permute-start = (bf16[512,3072]{1,0:T(8,128)(2,1)}, bf16[512,3072]{1,0:T(8,128)(2,1)}, u32[]{:S(2)}, u32[]{:S(2)}) collective-permute-start(bf16[512,3072]{1,0:T(8,128)(2,1)} %convolution_convert_fusion.1), channel_id=1, source_target_pairs={{0,8},{8,0},{16,24},{24,16},{1,9},{9,1},{17,25},{25,17},{2,10},{10... | collective-permute-start | bytes 9437192 | tf_op jit(solution)/shard_map/ppermute | solution.py:95
  362.1 34.5 %collective-permute-start.1 = (bf16[512,3072]{1,0:T(8,128)(2,1)}, bf16[512,3072]{1,0:T(8,128)(2,1)}, u32[]{:S(2)}, u32[]{:S(2)}) collective-permute-start(bf16[512,3072]{1,0:T(8,128)(2,1)} %convolution_convert_fusion), channel_id=1, source_target_pairs={{0,8},{8,0},{16,24},{24,16},{1,9},{9,1},{17,25},{25,17},{2,10},{10... | collective-permute-start | bytes 9437192 | tf_op jit(solution)/shard_map/ppermute | solution.py:95
  362.3 39.8 %collective-permute-start.2 = (bf16[1536,1024]{1,0:T(8,128)(2,1)}, bf16[1536,1024]{1,0:T(8,128)(2,1)}, u32[]{:S(2)}, u32[]{:S(2)}) collective-permute-start(bf16[1536,1024]{1,0:T(8,128)(2,1)} %convolution_convert_fusion.2), channel_id=1, source_target_pairs={{0,8},{8,0},{16,24},{24,16},{1,9},{9,1},{17,25},{25,17},{2,10},{10... | collective-permute-start | bytes 9437192 | tf_op jit(solution)/shard_map/ppermute | solution.py:95
  362.6 7.7 slice-start.2
  365.2 21.5 %collective-permute-start.9 = (bf16[1024,1024]{1,0:T(8,128)(2,1)}, bf16[1024,1024]{1,0:T(8,128)(2,1)}, u32[]{:S(2)}, u32[]{:S(2)}) collective-permute-start(bf16[1024,1024]{1,0:T(8,128)(2,1)} %convolution_convert_fusion.5), channel_id=1, source_target_pairs={{0,8},{8,0},{16,24},{24,16},{1,9},{9,1},{17,25},{25,17},{2,10},{10... | collective-permute-start | bytes 6291464 | tf_op jit(solution)/shard_map/ppermute | solution.py:95
  391.0 5.5 copy-start.101
  396.6 5.5 copy-start.57
  432.5 37.5 %collective-permute-start.11 = (bf16[256,3072]{1,0:T(8,128)(2,1)}, bf16[256,3072]{1,0:T(8,128)(2,1)}, u32[]{:S(2)}, u32[]{:S(2)}) collective-permute-start(bf16[256,3072]{1,0:T(8,128)(2,1)} %dynamic-slice_bitcast_fusion.2), channel_id=1, source_target_pairs={{0,16},{8,24},{16,0},{24,8},{1,17},{9,25},{17,1},{25,9},{2,18},{10... | collective-permute-start | bytes 4718600 | tf_op jit(solution)/shard_map/ppermute | solution.py:104
  434.8 68.9 %collective-permute-start.12 = (bf16[256,3072]{1,0:T(8,128)(2,1)}, bf16[256,3072]{1,0:T(8,128)(2,1)}, u32[]{:S(2)}, u32[]{:S(2)}) collective-permute-start(bf16[256,3072]{1,0:T(8,128)(2,1)} %dynamic-slice_bitcast_fusion.1), channel_id=1, source_target_pairs={{0,16},{8,24},{16,0},{24,8},{1,17},{9,25},{17,1},{25,9},{2,18},{10... | collective-permute-start | bytes 4718600 | tf_op jit(solution)/shard_map/ppermute | solution.py:104
  437.0 99.7 %collective-permute-start.13 = (bf16[768,1024]{1,0:T(8,128)(2,1)}, bf16[768,1024]{1,0:T(8,128)(2,1)}, u32[]{:S(2)}, u32[]{:S(2)}) collective-permute-start(bf16[768,1024]{1,0:T(8,128)(2,1)} %dynamic-slice_bitcast_fusion), channel_id=1, source_target_pairs={{0,16},{8,24},{16,0},{24,8},{1,17},{9,25},{17,1},{25,9},{2,18},{10... | collective-permute-start | bytes 4718600 | tf_op jit(solution)/shard_map/ppermute | solution.py:104
  441.4 7.4 copy-start.3
  441.5 7.4 copy-start.15
  441.5 7.4 copy-start.16
  441.5 7.4 copy-start.72
  441.5 7.4 copy-start.88
  454.5 49.2 %copy-start.37 = (bf16[512,3072]{1,0:T(8,128)(2,1)S(1)}, bf16[512,3072]{1,0:T(8,128)(2,1)}, u32[]{:S(2)}) copy-start(bf16[512,3072]{1,0:T(8,128)(2,1)} %add_convert_fusion.1) | copy-start | bytes 9437188
  454.5 100.3 %collective-permute-start.3 = (bf16[512,2048]{1,0:T(8,128)(2,1)}, bf16[512,2048]{1,0:T(8,128)(2,1)}, u32[]{:S(2)}, u32[]{:S(2)}) collective-permute-start(bf16[512,2048]{1,0:T(8,128)(2,1)} %convolution_convert_fusion.4), channel_id=1, source_target_pairs={{0,8},{8,0},{16,24},{24,16},{1,9},{9,1},{17,25},{25,17},{2,10},{10... | collective-permute-start | bytes 6291464 | tf_op jit(solution)/shard_map/ppermute | solution.py:95
  473.6 63.1 %copy-start.39 = (bf16[1536,1024]{1,0:T(8,128)(2,1)S(1)}, bf16[1536,1024]{1,0:T(8,128)(2,1)}, u32[]{:S(2)}) copy-start(bf16[1536,1024]{1,0:T(8,128)(2,1)} %add_convert_fusion) | copy-start | bytes 9437188
  540.0 305.3 %all-reduce.10.cloned.1.call-start = ((), (), s32[]{:S(2)}) async-start(), calls=%async_computation.7 | async-start | bytes 6291456 | tf_op jit(solution)/shard_map/psum | solution.py:358
  544.8 8.2 collective-permute-start.5
  545.7 26.1 %collective-permute-start.10 = (bf16[512,1024]{1,0:T(8,128)(2,1)S(1)}, bf16[512,1024]{1,0:T(8,128)(2,1)S(1)}, u32[]{:S(2)}, u32[]{:S(2)}) collective-permute-start(bf16[512,1024]{1,0:T(8,128)(2,1)S(1)} %dynamic-slice_bitcast_fusion.3), channel_id=1, source_target_pairs={{0,16},{8,24},{16,0},{24,8},{1,17},{9,25},{17,1},{25,9},{2,18},{10... | collective-permute-start | bytes 3145736 | tf_op jit(solution)/shard_map/ppermute | solution.py:104
  547.0 12.0 %collective-permute-start.7 = (bf16[512,1024]{1,0:T(8,128)(2,1)S(1)}, bf16[512,1024]{1,0:T(8,128)(2,1)S(1)}, u32[]{:S(2)}, u32[]{:S(2)}) collective-permute-start(bf16[512,1024]{1,0:T(8,128)(2,1)S(1)} %convolution_convert_fusion.7), channel_id=1, source_target_pairs={{0,8},{8,0},{16,24},{24,16},{1,9},{9,1},{17,25},{25,17},{2,10},{10... | collective-permute-start | bytes 3145736 | tf_op jit(solution)/shard_map/ppermute | solution.py:95
  553.8 29.3 %collective-permute-start.6 = (bf16[256,1024]{1,0:T(8,128)(2,1)S(1)}, bf16[256,1024]{1,0:T(8,128)(2,1)S(1)}, u32[]{:S(2)}, u32[]{:S(2)}) collective-permute-start(bf16[256,1024]{1,0:T(8,128)(2,1)S(1)} %dynamic-slice_bitcast_fusion.6), channel_id=1, source_target_pairs={{0,16},{8,24},{16,0},{24,8},{1,17},{9,25},{17,1},{25,9},{2,18},{10... | collective-permute-start | bytes 1572872 | tf_op jit(solution)/shard_map/ppermute | solution.py:104
  557.9 58.6 %collective-permute-start.4 = (bf16[256,2048]{1,0:T(8,128)(2,1)S(1)}, bf16[256,2048]{1,0:T(8,128)(2,1)S(1)}, u32[]{:S(2)}, u32[]{:S(2)}) collective-permute-start(bf16[256,2048]{1,0:T(8,128)(2,1)S(1)} %dynamic-slice_bitcast_fusion.4), channel_id=1, source_target_pairs={{0,16},{8,24},{16,0},{24,8},{1,17},{9,25},{17,1},{25,9},{2,18},{10... | collective-permute-start | bytes 3145736 | tf_op jit(solution)/shard_map/ppermute | solution.py:104
  559.8 55.7 %collective-permute-start.8 = (bf16[256,1024]{1,0:T(8,128)(2,1)S(1)}, bf16[256,1024]{1,0:T(8,128)(2,1)S(1)}, u32[]{:S(2)}, u32[]{:S(2)}) collective-permute-start(bf16[256,1024]{1,0:T(8,128)(2,1)S(1)} %dynamic-slice_bitcast_fusion.5), channel_id=1, source_target_pairs={{0,16},{8,24},{16,0},{24,8},{1,17},{9,25},{17,1},{25,9},{2,18},{10... | collective-permute-start | bytes 1572872 | tf_op jit(solution)/shard_map/ppermute | solution.py:104
  617.9 92.7 %copy-start.9 = (bf16[512,1024]{1,0:T(8,128)(2,1)S(1)}, bf16[512,1024]{1,0:T(8,128)(2,1)}, u32[]{:S(2)}) copy-start(bf16[512,1024]{1,0:T(8,128)(2,1)} %param.26) | copy-start | bytes 3145732
  617.9 92.7 %copy-start.76 = (f32[4,1,256]{2,1,0:T(1,128)S(1)}, f32[4,1,256]{2,1,0:T(1,128)}, u32[]{:S(2)}) copy-start(f32[4,1,256]{2,1,0:T(1,128)} %copy-done.75) | copy-start | bytes 12292
  617.9 92.8 %copy-start.80 = (f32[512]{0:T(512)S(1)}, f32[512]{0:T(512)}, u32[]{:S(2)}) copy-start(f32[512]{0:T(512)} %copy-done.79) | copy-start | bytes 6148
  710.6 8.5 copy-start.89
  710.6 52.9 %copy-start.17 = (f32[512,1024]{1,0:T(8,128)S(1)}, f32[512,1024]{1,0:T(8,128)}, u32[]{:S(2)}) copy-start(f32[512,1024]{1,0:T(8,128)} %get-tuple-element.143) | copy-start | bytes 6291460
  (72 other events, 222.1 us)
Sparse Core Ops, SparseCore 0:
  9.6 25.4 all-gather.9
  36.6 22.5 all-gather.11
  60.8 34.4 all-gather.13
  96.7 34.4 all-gather.15
  132.6 46.3 all-gather.17
  180.5 46.3 all-gather.19
  228.5 46.3 all-gather.21
  540.2 170.3 all-reduce.11
  715.0 130.3 all-reduce.9
